TPU v7x, 32 devices: a whole 2x2x4 slice. The times are simulated.
32 devices in a mesh: gx: 4 (over y, core), gy: 8 (over z, x).
Axes of the slice: x: 2, y: 2, z: 4, core: 2. Of those that a mesh axis runs over, the one named last changes fastest.
Arguments:
- source_field: float32 [2048, 16, 256], P('gx', 'gy'), may hold values from -6 to 6
- permeability: float32 [2048, 16, 256], P('gx', 'gy'), may hold values from 0.3 to 3
- layer_ids: int32 [256], replicated, may hold values from 0 to 3, as said below
- inverse_fine: float32 [4, 2048, 512], P(None, 'gx'), as said below
- couple_fine: float32 [2, 4, 4], P(None, None, 'gx'), may hold values from 0.35 to 0.7
- inverse_coarse: float32 [4, 2048, 512], P(None, 'gx'), as said below
- couple_coarse: float32 [2, 4, 4], P(None, None, 'gx'), may hold values from 0.35 to 0.7
- owner_map: int32 [8, 1], replicated, may hold values from 0 to 1
Outputs:
- solution_fine: float32 [2048, 16, 256], P('gx', 'gy')
- residual_fine: float32 [2048, 16, 256], P('gx', 'gy')
- solution_coarse: float32 [2048, 8, 256], P('gx', 'gy')
Inputs may be any that keep to these rules, and one draw needn't show every extreme that they name: owner_map names the aggregate of each level-6 plane; every aggregate below 2 holds at least one plane. `layer_ids`: every rock type names the same number of z cells. `inverse_fine`: each block is a positive-definite dense matrix with a diagonal dominating each line solve's coupling. `inverse_coarse`: each block is a positive-definite dense matrix with a diagonal dominating each line solve's coupling.
All inputs are finite; a program needn't handle non-finite values.
Results may differ from a plain program's by a relative error of at most 0.00012.
Values sent between devices are 32-bit elements; how exact they have to be, the bound alone decides.
A program may use at most 128 MiB of HBM per device.

v0:
```python
import functools
import jax
import jax.numpy as jnp
from jax import lax
from jax.experimental import pallas as pl
from jax.experimental.pallas import tpu as pltpu
from jax.sharding import PartitionSpec as P

NSWEEP = 3
WEIGHTS = (0.5, 0.15, 0.05)
STORAGE = 0.1
F32 = jnp.float32
BF16 = jnp.bfloat16
MESH = pl.DeviceIdType.MESH


def face(weight, one, two):
    return weight * 2.0 * one * two / (one + two)


def gains(rows):
    gain = jnp.zeros_like(rows[0][0])
    out = []
    for low_first, low_last, high_first, high_last in rows:
        inv = 1.0 / (1.0 - low_first * gain)
        link = high_first * inv
        back = low_last * gain
        gain = high_last + back * link
        out.append((low_first, low_last, inv, link, back, gain))
    return out


def chain(values, parts, own):
    count = len(parts)
    carry = jnp.zeros_like(values[0][0])
    firsts, lasts = [], []
    for (head, tail), (low_first, low_last, inv, link, back, gain) in zip(values, parts):
        first = (head - low_first * carry) * inv
        carry = tail - low_last * carry + back * first
        firsts.append(first)
        lasts.append(carry)
    following = jnp.zeros_like(carry)
    previous, after = following, following
    for p in range(count - 1, -1, -1):
        after = jnp.where(own == p, following, after)
        end = lasts[p] - parts[p][5] * following
        previous = jnp.where(own == p + 1, end, previous)
        following = firsts[p] - parts[p][3] * following
    return previous, after


def kernel(n, m, src, k, inv_f, inv_c, edge, coef, ids, same, u_out, r_out, c_out,
           hi, lo, g_hi, g_lo, val, halo, u_s, u_h, r_s, txb, txa, tzb, tza, ty,
           coefs, vals, sm, got, mix, back, h_send, h_recv, g_send, g_recv, a_send, a_recv):
    gx, gy = lax.axis_index("gx"), lax.axis_index("gy")
    width, depth = val.shape[1:]
    layers = hi.shape[0]
    planes = [slice(0, depth), slice(depth, 2 * depth)]
    row = lax.broadcasted_iota(jnp.int32, (width, depth), 0)
    lane = lax.broadcasted_iota(jnp.int32, (width, depth), 1)

    def halo_copy(kind, way, source):
        peer = gy + 1 if way == 0 else gy - 1
        return pltpu.make_async_remote_copy(
            src_ref=source, dst_ref=halo.at[kind, way],
            send_sem=h_send.at[kind, way], recv_sem=h_recv.at[kind, way],
            device_id={"gy": peer}, device_id_type=MESH)

    def can_send(way):
        return gy < m - 1 if way == 0 else gy > 0

    def comes(way):
        return gy > 0 if way == 0 else gy < m - 1

    def send_halo(kind, way, source):
        @pl.when(can_send(way))
        def _():
            halo_copy(kind, way, source).start()

    def wait_halo(kind, way, source):
        @pl.when(comes(way))
        def _():
            halo_copy(kind, way, source).wait_recv()

    def sent_halo(kind, way, source):
        @pl.when(can_send(way))
        def _():
            halo_copy(kind, way, source).wait_send()

    def gather(i, ref):
        out = []
        for d in range(1, n):
            out.append(pltpu.make_async_remote_copy(
                src_ref=ref.at[gx + 1], dst_ref=ref.at[gx + 1],
                send_sem=g_send.at[i, d - 1], recv_sem=g_recv.at[i, d - 1],
                device_id={"gx": lax.rem(gx + d, n)}, device_id_type=MESH))
        return out

    barrier = pltpu.get_barrier_semaphore()
    for d in range(1, n):
        pl.semaphore_signal(barrier, inc=1, device_id={"gx": lax.rem(gx + d, n)}, device_id_type=MESH)
    for d in range(1, m):
        pl.semaphore_signal(barrier, inc=1, device_id={"gy": lax.rem(gy + d, m)}, device_id_type=MESH)

    zero_rows = jnp.zeros(coefs.shape[1:], F32)
    coefs[0] = zero_rows
    coefs[n + 1] = zero_rows
    coefs[gx + 1, 0:8] = coef[...]
    for y in range(2):
        coefs[gx + 1, 8 + y : 9 + y] = k[0:1, planes[y]]
        coefs[gx + 1, 10 + y : 11 + y] = k[width - 1 : width, planes[y]]
    for way in range(2):
        @pl.when(jnp.logical_not(comes(way)))
        def _():
            for kind in range(4):
                halo[kind, way] = jnp.zeros((width, depth), F32)

    pl.semaphore_wait(barrier, n + m - 2)
    ends_of = [planes[1], planes[0]]
    for kind, ref in ((0, src), (1, k)):
        for way in range(2):
            send_halo(kind, way, ref.at[:, ends_of[way]])
    first_gather = gather(0, coefs)
    for c in first_gather:
        c.start()

    def split_matrices(ref):
        def body(i, _):
            b = ref[i]
            h = b.astype(BF16)
            hi[i] = h
            lo[i] = (b - h.astype(F32)).astype(BF16)
            return 0
        lax.fori_loop(0, layers, body, 0)

    def multiply(field, slot):
        h = field.astype(BF16)
        g_hi[...] = h
        g_lo[...] = (field - h.astype(F32)).astype(BF16)

        def body(i, _):
            v = jnp.dot(hi[i], g_hi[...], preferred_element_type=F32)
            v = v + jnp.dot(hi[i], g_lo[...], preferred_element_type=F32)
            v = v + jnp.dot(lo[i], g_hi[...], preferred_element_type=F32)
            val[slot] = jnp.where(ids[...] == i, v, val[slot])
            return 0

        val[slot] = jnp.zeros((width, depth), F32)
        lax.fori_loop(0, layers, body, 0)

    def solve_ends(i, slots, parts):
        for s in slots:
            vals[i, gx + 1, s : s + 1] = val[s, 0:1]
            vals[i, gx + 1, 4 + s : 5 + s] = val[s, width - 1 : width]
        copies = gather(1 + i, vals.at[i])
        for c in copies:
            c.start()
        for c in copies:
            c.wait_recv()
        count = len(slots)
        values = [(vals[i, p + 1, 0:count], vals[i, p + 1, 4 : 4 + count]) for p in range(n)]
        previous, after = chain(values, parts, gx)
        return previous, after, copies

    def edge_columns(base):
        out = []
        for side in range(2):
            at = base + side * layers
            total = jnp.zeros((width, depth), F32)
            for i in range(layers):
                total = jnp.where(ids[...] == i, edge[:, at + i : at + i + 1], total)
            out.append(total)
        return out

    def corrected(s, previous, after, base):
        low, high = edge_columns(base)
        return val[s] - previous[s : s + 1] * low - after[s : s + 1] * high

    split_matrices(inv_f)
    for y in range(2):
        multiply(src[:, planes[y]], y)
    for c in first_gather:
        c.wait_recv()
    every = [[coefs[p + 1, i : i + 1] for i in range(8)] for p in range(n)]
    parts_fine = gains([e[:4] for e in every])
    parts_coarse = gains([e[4:] for e in every])

    for y in range(2):
        kc = k[:, planes[y]]
        before = jnp.where(row == 0, coefs[gx, 10 + y : 11 + y], pltpu.roll(kc, 1, 0))
        after = jnp.where(row == width - 1, coefs[gx + 2, 8 + y : 9 + y], pltpu.roll(kc, width - 1, 0))
        txb[y] = face(WEIGHTS[0], kc, before)
        txa[y] = face(WEIGHTS[0], kc, after)
        tzb[y] = jnp.where(lane == 0, 0.0, face(WEIGHTS[2], kc, pltpu.roll(kc, 1, 1)))
        tza[y] = jnp.where(lane == depth - 1, 0.0, face(WEIGHTS[2], kc, pltpu.roll(kc, depth - 1, 1)))
    ty[1] = face(WEIGHTS[1], k[:, planes[0]], k[:, planes[1]])

    for way in range(2):
        wait_halo(0, way, src.at[:, ends_of[way]])
        multiply(halo[0, way], 2 + way)
    previous, after, sent0 = solve_ends(0, [0, 1, 2, 3], parts_fine)
    for y in range(2):
        u_s[0, y] = corrected(y, previous, after, 0)
    for way in range(2):
        u_h[way] = corrected(2 + way, previous, after, 0)
    sums = [previous[0:2], after[0:2]]
    all_sent = [first_gather, sent0]

    for way in range(2):
        wait_halo(1, way, k.at[:, ends_of[way]])
        ty[2 * way] = face(WEIGHTS[1], halo[1, way], k[:, planes[way]])

    def inner_residual(t, y):
        u = u_s[t, y]
        before = jnp.where(row == 0, sums[0][y : y + 1], pltpu.roll(u, 1, 0))
        after = jnp.where(row == width - 1, sums[1][y : y + 1], pltpu.roll(u, width - 1, 0))
        total = STORAGE * u + txb[y] * (u - before) + txa[y] * (u - after)
        total = total + ty[1] * (u - u_s[t, 1 - y])
        total = total + tzb[y] * (u - pltpu.roll(u, 1, 1)) + tza[y] * (u - pltpu.roll(u, depth - 1, 1))
        r_s[y] = src[:, planes[y]] - total

    def outer_residual(t, y, beside):
        return r_s[y] - ty[2 * y] * (u_s[t, y] - beside)

    for t in range(1, NSWEEP):
        for y in range(2):
            inner_residual(t - 1, y)
        for y in range(2):
            if t == 1:
                beside = u_h[y]
            else:
                wait_halo(t, y, u_s.at[t - 1, 1 - y])
                beside = halo[t, y]
            multiply(outer_residual(t - 1, y, beside), y)
        previous, after, more = solve_ends(t, [0, 1], parts_fine)
        all_sent.append(more)
        sums = [sums[0] + previous, sums[1] + after]
        for way in range(2):
            y = 1 - way
            u_s[t, y] = u_s[t - 1, y] + corrected(y, previous, after, 0)
            send_halo(t + 1, way, u_s.at[t, y])
    split_matrices(inv_c)
    for y in range(2):
        inner_residual(NSWEEP - 1, y)
        u_out[:, planes[y]] = u_s[NSWEEP - 1, y]
    coarse = None
    for y in range(2):
        wait_halo(NSWEEP, y, u_s.at[NSWEEP - 1, 1 - y])
        r = outer_residual(NSWEEP - 1, y, halo[NSWEEP, y])
        r_out[:, planes[y]] = r
        coarse = r if coarse is None else 0.5 * (coarse + r)
    multiply(coarse, 0)
    previous, after, more = solve_ends(NSWEEP, [0], parts_coarse)
    all_sent.append(more)
    sm[...] = corrected(0, previous, after, 2 * layers).reshape(sm.shape)

    def exchange(i, source, target):
        out = []
        for d in range(1, m):
            peer = lax.rem(gy + d, m)
            out.append(pltpu.make_async_remote_copy(
                src_ref=source.at[peer], dst_ref=target.at[gy],
                send_sem=a_send.at[i, d - 1], recv_sem=a_recv.at[i, d - 1],
                device_id={"gy": peer}, device_id_type=MESH))
        for c in out:
            c.start()
        target[gy] = source[gy]
        for c in out:
            c.wait_recv()
        return out

    all_sent.append(exchange(0, sm, got))

    def mix_rows(j, _):
        def add(i, total):
            return total + same[j, i] * got[i]
        mix[j] = lax.fori_loop(0, m, add, jnp.zeros(got.shape[1:], F32))
        return 0

    lax.fori_loop(0, m, mix_rows, 0)
    all_sent.append(exchange(1, mix, back))
    c_out[...] = back[...]
    for copies in all_sent:
        for c in copies:
            c.wait_send()
    for kind, ref in ((0, src), (1, k)):
        for way in range(2):
            sent_halo(kind, way, ref.at[:, ends_of[way]])
    for t in range(1, NSWEEP):
        for way in range(2):
            sent_halo(t + 1, way, u_s.at[t, 1 - way])


def local(source, perm, layer_ids, inv_fine, cpl_fine, inv_coarse, cpl_coarse, owner_map):
    width, planes, depth = source.shape
    layers = inv_fine.shape[0]
    n, m = lax.axis_size("gx"), lax.axis_size("gy")

    def columns(matrix, couple):
        return [couple[0] * matrix[:, :, 0], couple[1] * matrix[:, :, -1]]

    sides = columns(inv_fine, cpl_fine) + columns(inv_coarse, cpl_coarse)
    edge = jnp.transpose(jnp.concatenate(sides, 0))
    rows = jnp.stack([s[:, at] for s in sides for at in (0, -1)])
    coef = jnp.zeros((rows.shape[0], depth), F32)
    for i in range(layers):
        coef = jnp.where(layer_ids == i, rows[:, i : i + 1], coef)
    owners = owner_map[:, 0]
    same = (owners[:, None] == owners[None, :]).astype(F32)
    chunk = (m, width // m, depth)
    plane = (width, depth)
    flat = (width, planes * depth)
    vmem = pl.BlockSpec(memory_space=pltpu.VMEM)
    u, r, c = pl.pallas_call(
        functools.partial(kernel, n, m),
        out_shape=[jax.ShapeDtypeStruct(flat, F32), jax.ShapeDtypeStruct(flat, F32), jax.ShapeDtypeStruct(chunk, F32)],
        in_specs=[vmem] * 7 + [pl.BlockSpec(memory_space=pltpu.SMEM)],
        out_specs=[vmem] * 3,
        scratch_shapes=[
            pltpu.VMEM(inv_fine.shape, BF16),
            pltpu.VMEM(inv_fine.shape, BF16),
            pltpu.VMEM(plane, BF16),
            pltpu.VMEM(plane, BF16),
            pltpu.VMEM((4,) + plane, F32),
            pltpu.VMEM((4, 2) + plane, F32),
            pltpu.VMEM((NSWEEP, 2) + plane, F32),
            pltpu.VMEM((2,) + plane, F32),
            pltpu.VMEM((2,) + plane, F32),
            pltpu.VMEM((2,) + plane, F32),
            pltpu.VMEM((2,) + plane, F32),
            pltpu.VMEM((2,) + plane, F32),
            pltpu.VMEM((2,) + plane, F32),
            pltpu.VMEM((3,) + plane, F32),
            pltpu.VMEM((n + 2, 16, depth), F32),
            pltpu.VMEM((NSWEEP + 1, n + 2, 8, depth), F32),
            pltpu.VMEM(chunk, F32),
            pltpu.VMEM(chunk, F32),
            pltpu.VMEM(chunk, F32),
            pltpu.VMEM(chunk, F32),
            pltpu.SemaphoreType.DMA((4, 2)),
            pltpu.SemaphoreType.DMA((4, 2)),
            pltpu.SemaphoreType.DMA((NSWEEP + 2, n - 1)),
            pltpu.SemaphoreType.DMA((NSWEEP + 2, n - 1)),
            pltpu.SemaphoreType.DMA((2, m - 1)),
            pltpu.SemaphoreType.DMA((2, m - 1)),
        ],
        compiler_params=pltpu.CompilerParams(collective_id=0, has_side_effects=True, vmem_limit_bytes=56 << 20),
    )(source.reshape(flat), perm.reshape(flat), inv_fine, inv_coarse, edge, coef, layer_ids[None], same)
    return u.reshape(source.shape), r.reshape(source.shape), c.reshape(width, 1, depth)


def solution(mesh):
    in_specs = (
        P("gx", "gy", None),
        P("gx", "gy", None),
        P(),
        P(None, "gx", None),
        P(None, None, "gx"),
        P(None, "gx", None),
        P(None, None, "gx"),
        P(),
    )
    out_specs = (P("gx", "gy", None), P("gx", "gy", None), P("gx", "gy", None))
    return jax.shard_map(local, mesh=mesh, in_specs=in_specs, out_specs=out_specs, check_vma=False)
```

profile of v0, /device:TPU:16, one launch (start us, length us, event | category | flops | bytes accessed | tf_op | source)
XLA Modules:
  0.0 177.1 jit_solution(12041732937670142567)
XLA Ops:
  0.6 0.0 copy-start
  0.6 0.8 slice_bitcast_fusion.3
  1.5 0.8 slice_bitcast_fusion.1
  2.3 0.7 broadcast_compare_fusion.3
  3.0 1.4 compare_convert_fusion.same
  4.4 2.3 %copy.37 = f32[64,8,2,256]{3,1,2,0:T(8,128)} copy(f32[64,8,2,256]{3,2,1,0:T(2,128)} %bitcast.35) | data formatting | bytes 2097152
  6.6 2.3 %copy.38 = f32[64,8,2,256]{3,1,2,0:T(8,128)} copy(f32[64,8,2,256]{3,2,1,0:T(2,128)} %bitcast.36) | data formatting | bytes 2097152
  8.9 0.0 copy-done
  8.9 0.4 fusion
  9.3 0.3 copy.33
  9.6 0.3 copy.34
  10.0 0.1 bitcast_multiply_fusion.2
  10.0 0.2 slice_reduce_fusion.8
  10.2 0.2 slice_reduce_fusion.10
  10.4 1.9 %fusion.1 = (f32[4,512,1]{2,1,0:T(8,128)S(1)}, f32[4,512,1]{2,1,0:T(8,128)S(1)}) fusion(f32[4,512,512]{2,1,0:T(8,128)} %inv_c.1), kind=kLoop, calls=%fused_computation.28 | loop fusion | bytes 32768 | tf_op jit(solution)/shard_map/slice | solution.py:300
  12.3 0.3 copy.35
  12.6 0.3 copy.36
  13.0 0.1 bitcast_multiply_fusion
  13.1 0.2 slice_reduce_fusion.4
  13.3 0.2 slice_reduce_fusion.6
  13.5 0.2 slice_reduce_fusion.3
  13.7 0.7 select_select_fusion.coef
  14.4 0.8 copy.31
  15.2 153.8 %shard_map.103 = (f32[512,512]{1,0:T(8,128)}, f32[512,512]{1,0:T(8,128)}, f32[8,64,256]{2,1,0:T(8,128)}) custom-call(f32[512,512]{1,0:T(8,128)} %bitcast.32, f32[512,512]{1,0:T(8,128)} %bitcast.33, f32[4,512,512]{2,1,0:T(8,128)} %inv_f.1, f32[4,512,512]{2,1,0:T(8,128)} %inv_c.1, f32[512,16]{1,0:T(8,128)} %bitcast.34, f32[8,256]{1,0:T(8,128)} %select_select_fusion.coef, ...), custom_call_target="tpu_custom_call" | custom-call | tf_op jit(solution)/shard_map/pallas_call | solution.py:314
  169.0 2.8 %reshape.28 = f32[512,2,256]{2,1,0:T(2,128)} reshape(f32[512,512]{1,0:T(8,128)} %get-tuple-element.6) | data formatting | bytes 2097152 | tf_op jit(solution)/shard_map/reshape | solution.py:349
  171.8 2.4 %copy.32 = f32[512,1,256]{2,1,0:T(1,128)} copy(f32[512,1,256]{2,0,1:T(8,128)} %bitcast.37) | data formatting | bytes 1048576
  174.2 2.8 %reshape.29 = f32[512,2,256]{2,1,0:T(2,128)} reshape(f32[512,512]{1,0:T(8,128)} %get-tuple-element.7) | data formatting | bytes 2097152 | tf_op jit(solution)/shard_map/reshape | solution.py:349
  (2 shorter events, 0.0 us)
Async XLA Ops:
  0.6 8.3 %copy-start = (f32[4,512,512]{2,1,0:T(8,128)S(1)}, f32[4,512,512]{2,1,0:T(8,128)}, u32[]{:S(2)}) copy-start(f32[4,512,512]{2,1,0:T(8,128)} %inv_f.1) | copy-start | bytes 12582916
where the time goes:
time: 177 us
  Pallas kernels  154 us (87%)
  local copies, waits for them, and re-layouts  19.7 us (11%)
  other arithmetic  2.92 us (2%)
    pallas_call x1, Pallas kernels, local(): pl.pallas_call(functools.partial(kernel, n, m), out_shape=[jax.ShapeDtype...  154 us
    unnamed x9, local copies, waits for them, and re-layouts  8.24 us

commit v1 on v0

--- a/solution.py
+++ b/solution.py
@@ -49,9 +49,9 @@
     return previous, after
 
 
-def kernel(n, m, src, k, inv_f, inv_c, edge, coef, ids, same, u_out, r_out, c_out,
+def kernel(n, m, src, k, inv_f, inv_c, ids, cpl_f, cpl_c, same, u_out, r_out, c_out,
            hi, lo, g_hi, g_lo, val, halo, u_s, u_h, r_s, txb, txa, tzb, tza, ty,
-           coefs, vals, sm, got, mix, back, h_send, h_recv, g_send, g_recv, a_send, a_recv):
+           coefs, vals, sm, got, mix, back, cols, h_send, h_recv, g_send, g_recv, a_send, a_recv):
     gx, gy = lax.axis_index("gx"), lax.axis_index("gy")
     width, depth = val.shape[1:]
     layers = hi.shape[0]
@@ -105,7 +105,6 @@
     zero_rows = jnp.zeros(coefs.shape[1:], F32)
     coefs[0] = zero_rows
     coefs[n + 1] = zero_rows
-    coefs[gx + 1, 0:8] = coef[...]
     for y in range(2):
         coefs[gx + 1, 8 + y : 9 + y] = k[0:1, planes[y]]
         coefs[gx + 1, 10 + y : 11 + y] = k[width - 1 : width, planes[y]]
@@ -120,6 +119,16 @@
     for kind, ref in ((0, src), (1, k)):
         for way in range(2):
             send_halo(kind, way, ref.at[:, ends_of[way]])
+    for side in range(2):
+        at = (width - 1) * side
+        for base, inv, cpl in ((0, inv_f, cpl_f), (2, inv_c, cpl_c)):
+            total = jnp.zeros((width, depth), F32)
+            for i in range(layers):
+                total = jnp.where(ids[...] == i, cpl[side, i, 0] * inv[i, :, at : at + 1], total)
+            cols[base + side] = total
+    for i in range(4):
+        coefs[gx + 1, 2 * i : 2 * i + 1] = cols[i, 0:1]
+        coefs[gx + 1, 2 * i + 1 : 2 * i + 2] = cols[i, width - 1 : width]
     first_gather = gather(0, coefs)
     for c in first_gather:
         c.start()
@@ -162,19 +171,8 @@
         previous, after = chain(values, parts, gx)
         return previous, after, copies
 
-    def edge_columns(base):
-        out = []
-        for side in range(2):
-            at = base + side * layers
-            total = jnp.zeros((width, depth), F32)
-            for i in range(layers):
-                total = jnp.where(ids[...] == i, edge[:, at + i : at + i + 1], total)
-            out.append(total)
-        return out
-
     def corrected(s, previous, after, base):
-        low, high = edge_columns(base)
-        return val[s] - previous[s : s + 1] * low - after[s : s + 1] * high
+        return val[s] - previous[s : s + 1] * cols[base] - after[s : s + 1] * cols[base + 1]
 
     split_matrices(inv_f)
     for y in range(2):
@@ -252,7 +250,7 @@
     multiply(coarse, 0)
     previous, after, more = solve_ends(NSWEEP, [0], parts_coarse)
     all_sent.append(more)
-    sm[...] = corrected(0, previous, after, 2 * layers).reshape(sm.shape)
+    sm[...] = corrected(0, previous, after, 2).reshape(sm.shape)
 
     def exchange(i, source, target):
         out = []
@@ -293,18 +291,7 @@
 
 def local(source, perm, layer_ids, inv_fine, cpl_fine, inv_coarse, cpl_coarse, owner_map):
     width, planes, depth = source.shape
-    layers = inv_fine.shape[0]
     n, m = lax.axis_size("gx"), lax.axis_size("gy")
-
-    def columns(matrix, couple):
-        return [couple[0] * matrix[:, :, 0], couple[1] * matrix[:, :, -1]]
-
-    sides = columns(inv_fine, cpl_fine) + columns(inv_coarse, cpl_coarse)
-    edge = jnp.transpose(jnp.concatenate(sides, 0))
-    rows = jnp.stack([s[:, at] for s in sides for at in (0, -1)])
-    coef = jnp.zeros((rows.shape[0], depth), F32)
-    for i in range(layers):
-        coef = jnp.where(layer_ids == i, rows[:, i : i + 1], coef)
     owners = owner_map[:, 0]
     same = (owners[:, None] == owners[None, :]).astype(F32)
     chunk = (m, width // m, depth)
@@ -314,7 +301,7 @@
     u, r, c = pl.pallas_call(
         functools.partial(kernel, n, m),
         out_shape=[jax.ShapeDtypeStruct(flat, F32), jax.ShapeDtypeStruct(flat, F32), jax.ShapeDtypeStruct(chunk, F32)],
-        in_specs=[vmem] * 7 + [pl.BlockSpec(memory_space=pltpu.SMEM)],
+        in_specs=[vmem] * 5 + [pl.BlockSpec(memory_space=pltpu.SMEM)] * 3,
         out_specs=[vmem] * 3,
         scratch_shapes=[
             pltpu.VMEM(inv_fine.shape, BF16),
@@ -337,6 +324,7 @@
             pltpu.VMEM(chunk, F32),
             pltpu.VMEM(chunk, F32),
             pltpu.VMEM(chunk, F32),
+            pltpu.VMEM((4,) + plane, F32),
             pltpu.SemaphoreType.DMA((4, 2)),
             pltpu.SemaphoreType.DMA((4, 2)),
             pltpu.SemaphoreType.DMA((NSWEEP + 2, n - 1)),
@@ -345,7 +333,7 @@
             pltpu.SemaphoreType.DMA((2, m - 1)),
         ],
         compiler_params=pltpu.CompilerParams(collective_id=0, has_side_effects=True, vmem_limit_bytes=56 << 20),
-    )(source.reshape(flat), perm.reshape(flat), inv_fine, inv_coarse, edge, coef, layer_ids[None], same)
+    )(source.reshape(flat), perm.reshape(flat), inv_fine, inv_coarse, layer_ids[None], cpl_fine, cpl_coarse, same)
     return u.reshape(source.shape), r.reshape(source.shape), c.reshape(width, 1, depth)
 
 

time: 177 us -> 173 us (0.977); the launches traced: 177 us -> 170 us
  local copies, waits for them, and re-layouts: 19.7 us -> 15.3 us
  Pallas kernels: 154 us -> 152 us
    slice x7 -> x0, local copies, waits for them, and re-layouts: 3.23 us -> none  [the longest x2 2.28 us: columns(): return [couple[0] * matrix[:, :, 0], couple[1] * matrix[:, :, -1]]]
    unnamed x9 -> x5, local copies, waits for them, and re-layouts: 8.24 us -> 9.61 us
where the time goes in v1:
time: 173 us; the launch traced here: 170 us
  Pallas kernels  152 us (88%)
  local copies, waits for them, and re-layouts  15.3 us (9%)
    pallas_call x1, Pallas kernels, local(): pl.pallas_call(functools.partial(kernel, n, m), out_shape=[jax.ShapeDtype...  152 us
    unnamed x5, local copies, waits for them, and re-layouts  9.61 us

profile of v1, /device:TPU:16, one launch (start us, length us, event | category | flops | bytes accessed | tf_op | source)
XLA Modules:
  0.0 169.6 jit_solution(6252694482809259469)
XLA Ops:
  0.6 1.4 copy.11.cpl_f
  2.0 1.4 copy.12.cpl_c
  3.3 1.4 compare_convert_fusion.same
  4.7 2.3 %copy.14 = f32[64,8,2,256]{3,1,2,0:T(8,128)} copy(f32[64,8,2,256]{3,2,1,0:T(2,128)} %bitcast.9) | data formatting | bytes 2097152
  7.0 2.3 %copy.15 = f32[64,8,2,256]{3,1,2,0:T(8,128)} copy(f32[64,8,2,256]{3,2,1,0:T(2,128)} %bitcast.10) | data formatting | bytes 2097152
  9.3 152.2 %shard_map.103 = (f32[512,512]{1,0:T(8,128)}, f32[512,512]{1,0:T(8,128)}, f32[8,64,256]{2,1,0:T(8,128)}) custom-call(f32[512,512]{1,0:T(8,128)} %bitcast.7, f32[512,512]{1,0:T(8,128)} %bitcast.8, f32[4,512,512]{2,1,0:T(8,128)} %inv_f.1, f32[4,512,512]{2,1,0:T(8,128)} %inv_c.1, s32[1,256]{1,0:T(1,128)} %bitcast.13, f32[2,4,1]{2,1,0:T(4,128)} %copy.11.cpl_f, ...), custom_call_target="tpu_custom_call" | custom-call | tf_op jit(solution)/shard_map/pallas_call | solution.py:301
  161.5 2.8 %reshape.24 = f32[512,2,256]{2,1,0:T(2,128)} reshape(f32[512,512]{1,0:T(8,128)} %get-tuple-element.6) | data formatting | bytes 2097152 | tf_op jit(solution)/shard_map/reshape | solution.py:337
  164.3 2.4 %copy.13 = f32[512,1,256]{2,1,0:T(1,128)} copy(f32[512,1,256]{2,0,1:T(8,128)} %bitcast.11) | data formatting | bytes 1048576
  166.7 2.8 %reshape.25 = f32[512,2,256]{2,1,0:T(2,128)} reshape(f32[512,512]{1,0:T(8,128)} %get-tuple-element.7) | data formatting | bytes 2097152 | tf_op jit(solution)/shard_map/reshape | solution.py:337
